TPU v7x, 32 devices: a whole 2x2x4 slice. The times are simulated.
32 devices in a mesh: grp: 2 (over y), row: 4 (over z), col: 2 (over x), sub: 2 (over core).
Axes of the slice: x: 2, y: 2, z: 4, core: 2. Of those that a mesh axis runs over, the one named last changes fastest.
Arguments:
- samples: bfloat16 [512, 2, 16, 512], P(('grp', 'row', 'col', 'sub')), parts along dimension 0, may hold values from -6 to 6
- analysis_taps: float32 [16, 16], replicated, may hold values from -1 to 1
- synthesis_taps: float32 [16, 16], replicated, may hold values from -1 to 1
- antenna_station: int32 [512], P('grp'), parts along dimension 0, may hold values from 0 to 31, as said below
- station_group: int32 [64, 1], P('grp'), parts along dimension 0, may hold values from 0 to 7
- beam_group: int32 [2048], P('grp'), parts along dimension 0, may hold values from 0 to 7
- beam_weights: bfloat16 [32, 2, 1024, 32], P(('grp', 'row'), None, ('col', 'sub')), parts along dimension 0, may hold values from -6 to 6
Outputs:
- visibilities: float32 [16, 2, 64, 32], P('row', None, ('grp', 'col', 'sub')), parts along dimension 2
- beam_series: float32 [2048, 2, 16, 512], P(('grp', 'col', 'sub', 'row')), parts along dimension 0
There are 2 independent parts, one for each index of `grp`. A program takes and returns all parts, laid end to end along the dimension named above; an argument that names none is the same for every part. Nothing has to cross between parts.
Inputs may be any that keep to these rules, and one draw needn't show every extreme that they name: `antenna_station`: every station is named by exactly 8 antennas.
All inputs are finite; a program needn't handle non-finite values.
Results may differ from a plain program's by a relative error of at most 0.005.
Values may be sent and summed in bfloat16 or wider, within the bound.
A program may use at most 64 MiB of HBM per device.

v0:
```python
import math
import jax
import jax.numpy as jnp
from jax import lax
from jax.sharding import PartitionSpec as P

ANTENNAS_PER_STN = 8
SPEC = 512


def polyphase(signal, coefficients):
    length = signal.shape[-1]
    output = coefficients[0][:, None] * signal
    for tap_index in range(1, coefficients.shape[0]):
        shifted = jnp.pad(
            signal[..., : length - tap_index], [(0, 0)] * (signal.ndim - 1) + [(tap_index, 0)]
        )
        output = output + coefficients[tap_index][:, None] * shifted
    return output


def fourier_table(length, direction):
    indices = jnp.arange(length)
    angles = (
        2.0 * math.pi / length * (indices[:, None] * indices[None, :] % length).astype(jnp.float32)
    )
    cosine_part = jnp.cos(angles)
    sine_part = jnp.sin(angles)
    table = jnp.stack(
        [
            jnp.stack([cosine_part, direction * sine_part]),
            jnp.stack([-direction * sine_part, cosine_part]),
        ]
    )
    return table.transpose(0, 2, 1, 3) * (1.0 / math.sqrt(length))


def body(
    samples, analysis_taps, synthesis_taps, antenna_station, station_group, beam_group, beam_weights
):
    high = lax.Precision.HIGHEST
    block_count = lax.axis_size(("col", "sub"))
    block_index = lax.axis_index(("col", "sub"))
    filtered = polyphase(samples.astype(jnp.float32), analysis_taps)
    spectra = jnp.einsum(
        "aqcf,qcpk->apkf", filtered, fourier_table(samples.shape[2], -1.0), precision=high
    ).astype(jnp.bfloat16)
    turned = lax.all_to_all(spectra, "row", split_axis=2, concat_axis=0, tiled=True)
    local_count = spectra.shape[0]
    held_rows = turned.shape[0]
    chan_rows = turned.shape[2]
    spec_len = turned.shape[3]
    station_count = station_group.shape[0]
    flat_width = 2 * chan_rows * spec_len
    tile_rows = station_count // block_count
    shard_rows = lax.all_gather(turned, ("col", "sub"), axis=0, tiled=True)
    row_total = shard_rows.shape[0]
    positions = jnp.arange(row_total, dtype=jnp.int32)
    source_block = positions // held_rows
    offset_rows = positions % held_rows
    source_row = offset_rows // local_count
    antenna = offset_rows % local_count
    global_index = (source_row * block_count + source_block) * local_count + antenna
    targets = antenna_station[global_index]
    wanted = jnp.arange(station_count, dtype=jnp.int32)
    one_hot = (targets[None, :] == wanted[:, None]).astype(jnp.bfloat16)
    summed_values = jnp.dot(
        one_hot, shard_rows.reshape(row_total, flat_width), preferred_element_type=jnp.float32
    )
    flat_stations = (summed_values * (1.0 / math.sqrt(ANTENNAS_PER_STN))).astype(jnp.bfloat16)
    station_list = flat_stations.reshape(station_count, 2, chan_rows, spec_len)
    real_part = station_list[:, 0]
    imag_part = station_list[:, 1]
    own_rows = lax.dynamic_slice_in_dim(station_list, block_index * tile_rows, tile_rows, 0)
    own_real = own_rows[:, 0]
    own_imag = own_rows[:, 1]
    vis_real = (
        jnp.einsum("icf,jcf->cij", own_real, real_part, preferred_element_type=jnp.float32)
        + jnp.einsum("icf,jcf->cij", own_imag, imag_part, preferred_element_type=jnp.float32)
    ) * (1.0 / SPEC)
    vis_imag = (
        jnp.einsum("icf,jcf->cij", own_imag, real_part, preferred_element_type=jnp.float32)
        - jnp.einsum("icf,jcf->cij", own_real, imag_part, preferred_element_type=jnp.float32)
    ) * (1.0 / SPEC)
    visibilities = jnp.stack([vis_real, vis_imag], axis=1)
    beam_block = beam_weights.shape[2]
    own_groups = lax.dynamic_slice_in_dim(beam_group, block_index * beam_block, beam_block, 0)
    members = station_group[:, 0][None, :] == own_groups[:, None]
    scaling = 1.0 / jnp.sqrt(jnp.sum(members.astype(jnp.float32), axis=1))
    weights = jnp.where(members[None, None], beam_weights, jnp.zeros((), jnp.bfloat16))
    weight_real = weights[:, 0]
    imaginary_weight = weights[:, 1]
    beam_real = jnp.einsum(
        "cbs,scf->bcf", weight_real, real_part, preferred_element_type=jnp.float32
    ) - jnp.einsum("cbs,scf->bcf", imaginary_weight, imag_part, preferred_element_type=jnp.float32)
    beam_imag = jnp.einsum(
        "cbs,scf->bcf", weight_real, imag_part, preferred_element_type=jnp.float32
    ) + jnp.einsum("cbs,scf->bcf", imaginary_weight, real_part, preferred_element_type=jnp.float32)
    beams = (jnp.stack([beam_real, beam_imag], axis=1) * scaling[:, None, None, None]).astype(
        jnp.bfloat16
    )
    returned = lax.all_to_all(beams, "row", split_axis=0, concat_axis=2, tiled=True)
    inverse = jnp.einsum(
        "bqkf,qkpc->bpcf",
        returned.astype(jnp.float32),
        fourier_table(returned.shape[2], 1.0),
        precision=high,
    )
    beam_series = polyphase(inverse, synthesis_taps)
    return (visibilities, beam_series)


def solution(mesh):
    return jax.shard_map(
        body,
        mesh=mesh,
        in_specs=(
            P(("grp", "row", "col", "sub"), None, None, None),
            P(),
            P(),
            P("grp"),
            P("grp", None),
            P("grp"),
            P(("grp", "row"), None, ("col", "sub"), None),
        ),
        out_specs=(
            P("row", None, ("grp", "col", "sub"), None),
            P(("grp", "col", "sub", "row"), None, None, None),
        ),
        check_vma=False,
    )
```

profile of v0, /device:TPU:0, one launch (start us, length us, event | category | flops | bytes accessed | tf_op | source)
XLA Modules:
  0.0 157.8 jit_solution(14489460331540854039)
XLA Ops:
  7.4 1.2 slice.274
  8.5 1.2 slice.275
  11.4 0.2 copy-done.3
  11.6 5.1 %fusion.3 = bf16[16,2,16,512]{3,2,0,1:T(8,128)(2,1)S(1)} fusion(f32[16,2,16,497]{3,2,1,0:T(8,128)S(1)} %slice.288, f32[16,2,16,498]{3,2,1,0:T(8,128)S(1)} %slice.287, f32[16,2,16,499]{3,2,1,0:T(8,128)S(1)} %slice.286, f32[16,2,16,500]{3,2,1,0:T(8,128)S(1)} %slice.285, f32[16,2,16,501]{3,2,1,0:T(8,128)S(1)} %slice.284, f32[16,2,16,502]{3,2,1,0:T(8,128)S(1)} %slice.283, ...), kind=kOutput, calls=%fused_computation.11 | convolution fusion | flops 109316096 | bytes 16536576 | tf_op jit(solution)/shard_map/aqcf,qcpk->apkf/dot_general | solution.py:45
  16.8 0.3 copy.55
  17.1 20.6 %all_to_all.36 = bf16[16,2,16,512]{3,0,1,2:T(8,128)(2,1)S(1)} all-to-all(bf16[16,2,16,512]{3,0,1,2:T(8,128)(2,1)S(1)} %copy.55), channel_id=1, replica_groups=mesh['grp'=2,'row'=4,'col'=2,'sub'=2] {'row'}, dimensions={2} | all-to-all | bytes 1048576 | tf_op jit(solution)/shard_map/all_to_all | solution.py:48
  37.7 0.8 copy.57
  38.5 0.8 dynamic_slice.7
  39.4 1.9 %gather_fusion = s32[256]{0:T(256)S(1)} fusion(s32[256]{0:T(256)S(1)} %copy-done, s32[1024]{0:T(1024)S(1)} %pad_clamp_fusion), kind=kCustom, calls=%fused_computation | custom fusion | bytes 3072 | tf_op jit(solution)/shard_map/gather | solution.py:64
  41.5 18.9 %all-gather.2.cloned.1.call-done = bf16[256,2,4,512]{3,0,2,1:T(8,128)(2,1)} async-done(((bf16[64,2,4,512]{3,0,2,1:T(8,128)(2,1)}), bf16[256,2,4,512]{3,0,2,1:T(8,128)(2,1)}) %all-gather.2.cloned.1.call-update) | async-done | bytes 2097168 | tf_op jit(solution)/shard_map/all_gather | solution.py:56
  60.4 2.8 %copy.58 = bf16[256,2,4,512]{0,3,2,1:T(8,128)(2,1)S(1)} copy(bf16[256,2,4,512]{3,0,2,1:T(8,128)(2,1)} %all-gather.2.cloned.1.call-done) | data formatting | bytes 4194304 | tf_op jit(solution)/shard_map/all_gather | solution.py:56
  63.2 0.7 fusion
  63.9 0.2 reshape.289
  64.2 0.5 fusion.72
  64.6 0.5 fusion.75
  65.1 0.5 subtract_bitcast_fusion
  65.6 0.5 add_bitcast_fusion
  66.1 0.4 fusion.1
  66.6 3.1 %copy.64 = bf16[256,2,4,512]{3,2,1,0:T(4,128)(2,1)} copy(bf16[256,2,4,512]{0,3,2,1:T(8,128)(2,1)S(1)} %fusion.1) | data formatting | bytes 4194304 | tf_op jit(solution)/shard_map/convert_element_type | solution.py:99
  69.6 4.6 %all-to-all-start.1 = ((bf16[256,2,4,512]{3,2,1,0:T(4,128)(2,1)}), bf16[256,2,4,512]{3,2,1,0:T(4,128)(2,1)S(1)}, u32[]{:S(2)}, u32[]{:S(2)}) async-start(bf16[256,2,4,512]{3,2,1,0:T(4,128)(2,1)} %copy.64), calls=%async_computation.1 | async-start | bytes 4194304 | tf_op jit(solution)/shard_map/all_to_all | solution.py:102
  74.3 0.1 fusion.74
  74.5 0.2 fusion.7
  74.6 0.1 fusion.73
  74.8 0.2 fusion.5
  74.9 0.6 copy.67
  75.6 47.3 %all-to-all-done.1 = bf16[256,2,4,512]{3,2,1,0:T(4,128)(2,1)S(1)} async-done(((bf16[256,2,4,512]{3,2,1,0:T(4,128)(2,1)}), bf16[256,2,4,512]{3,2,1,0:T(4,128)(2,1)S(1)}, u32[]{:S(2)}, u32[]{:S(2)}) %all-to-all-start.1) | async-done | bytes 2097184 | tf_op jit(solution)/shard_map/all_to_all | solution.py:102
  122.8 0.7 copy.65
  123.5 2.9 %copy.66 = bf16[64,2,4,4,512]{4,3,2,1,0:T(4,128)(2,1)} copy(bf16[64,2,4,4,512]{4,0,2,3,1:T(8,128)(2,1)S(1)} %bitcast.188) | data formatting | bytes 4194304 | tf_op jit(solution)/shard_map/all_to_all | solution.py:102
  126.5 2.5 %reshape.302 = bf16[64,2,16,512,1]{3,2,1,0,4:T(8,128)(2,1)S(1)} reshape(bf16[64,2,4,4,512]{4,3,2,1,0:T(4,128)(2,1)} %copy.66) | data formatting | bytes 4194304 | tf_op jit(solution)/shard_map/all_to_all | solution.py:102
  129.0 2.0 %convolution_bitcast_fusion = f32[64,2,16,512]{3,2,0,1:T(8,128)S(1)} fusion(bf16[64,2,16,512,1]{3,2,1,0,4:T(8,128)(2,1)S(1)} %reshape.302, f32[1,2,16,16]{2,3,0,1:T(8,128)S(1)} %get-tuple-element.37, f32[1,2,16,16]{2,3,0,1:T(8,128)S(1)} %get-tuple-element.16), kind=kOutput, calls=%fused_computation.6 | convolution fusion | flops 402655232 | bytes 6295552 | tf_op jit(solution)/shard_map/bqkf,qkpc->bpcf/dot_general | solution.py:103
  131.0 17.3 %multiply_add_fusion = f32[64,2,16,512]{3,2,0,1:T(8,128)S(1)} fusion(f32[64,2,16,497]{3,2,0,1:T(8,128)S(1)} %bitcast.172, f32[64,2,16,498]{3,2,0,1:T(8,128)S(1)} %bitcast.173, f32[64,2,16,499]{3,2,0,1:T(8,128)S(1)} %bitcast.174, f32[64,2,16,500]{3,2,0,1:T(8,128)S(1)} %bitcast.175, f32[64,2,16,501]{3,2,0,1:T(8,128)S(1)} %bitcast.176, ...), kind=kLoop, calls=%fused_computation.5 | loop fusion | flops 32505856 | bytes 70321152 | tf_op jit(solution)/shard_map/add | solution.py:18
  148.4 2.6 %copy.68 = f32[64,2,16,512]{3,2,1,0:T(8,128)} copy(f32[64,2,16,512]{3,2,0,1:T(8,128)S(1)} %multiply_add_fusion) | data formatting | bytes 8388608
  (40 shorter events, 2.2 us)
Async XLA Ops:
  7.2 32.3 %copy-start = (s32[256]{0:T(256)S(1)}, s32[256]{0:T(256)}, u32[]{:S(2)}) copy-start(s32[256]{0:T(256)} %param.10) | copy-start | bytes 3076
  7.2 2.5 %copy-start.1 = (bf16[16,2,16,512]{3,2,1,0:T(8,128)(2,1)S(1)}, bf16[16,2,16,512]{3,2,1,0:T(8,128)(2,1)}, u32[]{:S(2)}) copy-start(bf16[16,2,16,512]{3,2,1,0:T(8,128)(2,1)} %param.7) | copy-start | bytes 1572868
  7.2 53.2 %all-gather.2.cloned.1.call-start = ((), (), s32[]{:S(2)}) async-start(), calls=%async_computation.2 | async-start | bytes 2621440 | tf_op jit(solution)/shard_map/all_gather | solution.py:56
  10.9 0.7 copy-start.3
  11.6 27.7 %copy-start.5 = (s32[32,1]{0,1:T(1,128)S(1)}, s32[32,1]{0,1:T(1,128)}, u32[]{:S(2)}) copy-start(s32[32,1]{0,1:T(1,128)} %param.11) | copy-start | bytes 388
  16.7 24.7 %copy-start.2 = (bf16[4,2,256,32]{2,3,1,0:T(8,128)(2,1)S(1)}, bf16[4,2,256,32]{2,3,1,0:T(8,128)(2,1)}, u32[]{:S(2)}) copy-start(bf16[4,2,256,32]{2,3,1,0:T(8,128)(2,1)} %param.13) | copy-start | bytes 393220
  66.5 7.7 %copy-start.4 = (f32[16,16]{1,0:T(8,128)S(1)}, f32[16,16]{1,0:T(8,128)}, u32[]{:S(2)}) copy-start(f32[16,16]{1,0:T(8,128)} %param.9) | copy-start | bytes 3076
  69.6 53.2 %all-to-all-start.1 = ((bf16[256,2,4,512]{3,2,1,0:T(4,128)(2,1)}), bf16[256,2,4,512]{3,2,1,0:T(4,128)(2,1)S(1)}, u32[]{:S(2)}, u32[]{:S(2)}) async-start(bf16[256,2,4,512]{3,2,1,0:T(4,128)(2,1)} %copy.64), calls=%async_computation.1 | async-start | bytes 4194304 | tf_op jit(solution)/shard_map/all_to_all | solution.py:102
Sparse Core Ops, SparseCore 0:
  38.6 21.6 all-gather.1
where the time goes:
time: 158 us
  waiting for transfers between devices  66.2 us (42%)
  local copies, waits for them, and re-layouts  23.5 us (15%)
  blocking collectives  20.6 us (13%)
  other arithmetic  18.1 us (11%)
  between operations  14.4 us (9%)
  matrix products  10.3 us (7%)
  starting transfers between devices  4.66 us (3%)
    all_to_all x1, waiting for transfers between devices, body(): lax.all_to_all(beams, 'row', split_axis=0, concat_axis=2, tiled=True)  47.3 us
    all_to_all x1, blocking collectives, body(): lax.all_to_all(spectra, 'row', split_axis=2, concat_axis=0, tiled=True)  20.6 us
    all_gather x1, waiting for transfers between devices, body(): shard_rows = lax.all_gather(turned, ('col', 'sub'), axis=0, tiled=True)  18.9 us
    add x1, other arithmetic, polyphase(): output = output + coefficients[tap_index][:, None] * shifted  17.3 us
    all_to_all x3, local copies, waits for them, and re-layouts, body(): lax.all_to_all(beams, 'row', split_axis=0, concat_axis=2, tiled=True)  6.19 us
    dot_general x1, matrix products, body(): jnp.einsum('aqcf,qcpk->apkf', filtered, fourier_table(samples.shape[2], -...  5.12 us
    all_to_all x1, starting transfers between devices, body(): lax.all_to_all(beams, 'row', split_axis=0, concat_axis=2, tiled=True)  4.62 us
    slice x15, local copies, waits for them, and re-layouts, polyphase(): signal[..., :length - tap_index]  3.91 us
  transfers between devices with their start and end apart: 2, of which 2 were waited for; matrix products, arithmetic and copies ran while one was open for 3% of the time, Pallas kernels for 0%

commit v1 on v0

--- a/solution.py
+++ b/solution.py
@@ -6,6 +6,12 @@
 
 ANTENNAS_PER_STN = 8
 SPEC = 512
+
+
+def trade_parts(x, axis, split, join):
+    shards = jnp.split(x, lax.axis_size(axis), axis=split)
+    incoming = lax.all_to_all(jnp.stack(shards), axis, 0, 0)
+    return jnp.concatenate(incoming, axis=join)
 
 
 def polyphase(signal, coefficients):
@@ -99,7 +105,7 @@
     beams = (jnp.stack([beam_real, beam_imag], axis=1) * scaling[:, None, None, None]).astype(
         jnp.bfloat16
     )
-    returned = lax.all_to_all(beams, "row", split_axis=0, concat_axis=2, tiled=True)
+    returned = trade_parts(beams, "row", 0, 2)
     inverse = jnp.einsum(
         "bqkf,qkpc->bpcf",
         returned.astype(jnp.float32),

time: 158 us -> 152 us (0.962)
  local copies, waits for them, and re-layouts: 23.5 us -> 14.6 us
  other arithmetic: 18.1 us -> 19.9 us
    all_to_all x3 -> x0, local copies, waits for them, and re-layouts: 6.19 us -> none  [body(): lax.all_to_all(beams, 'row', split_axis=0, concat_axis=2, tiled=True)]
    convert_element_type x1 -> x0, local copies, waits for them, and re-layouts: 3.08 us -> none  [body(): (jnp.stack([beam_real, beam_imag], axis=1) * scaling[:, None, None, None]...]
    another operation x0 -> x1, other arithmetic: none -> 1.58 us  [trade_parts(): incoming = lax.all_to_all(jnp.stack(shards), axis, 0, 0)]
where the time goes in v1:
time: 152 us; the launch traced here: 151 us
  waiting for transfers between devices  66.2 us (44%)
  blocking collectives  20.6 us (14%)
  other arithmetic  19.9 us (13%)
  local copies, waits for them, and re-layouts  14.6 us (10%)
  between operations  14.4 us (9%)
  matrix products  11 us (7%)
  starting transfers between devices  4.63 us (3%)
    all_to_all x1, waiting for transfers between devices, trade_parts(): incoming = lax.all_to_all(jnp.stack(shards), axis, 0, 0)  47.3 us
    all_to_all x1, blocking collectives, body(): lax.all_to_all(spectra, 'row', split_axis=2, concat_axis=0, tiled=True)  20.6 us
    all_gather x1, waiting for transfers between devices, body(): shard_rows = lax.all_gather(turned, ('col', 'sub'), axis=0, tiled=True)  18.9 us
    add x1, other arithmetic, polyphase(): output = output + coefficients[tap_index][:, None] * shifted  17.3 us
    dot_general x1, matrix products, body(): jnp.einsum('aqcf,qcpk->apkf', filtered, fourier_table(samples.shape[2], -...  5.12 us
    all_to_all x1, starting transfers between devices, trade_parts(): incoming = lax.all_to_all(jnp.stack(shards), axis, 0, 0)  4.59 us
    slice x15, local copies, waits for them, and re-layouts, polyphase(): signal[..., :length - tap_index]  3.95 us
    unnamed x14, local copies, waits for them, and re-layouts  3.39 us
  transfers between devices with their start and end apart: 2, of which 2 were waited for; matrix products, arithmetic and copies ran while one was open for 3% of the time, Pallas kernels for 0%

profile of v1, /device:TPU:0, one launch (start us, length us, event | category | flops | bytes accessed | tf_op | source)
XLA Modules:
  0.0 151.4 jit_solution(508741926521402387)
XLA Ops:
  7.4 1.2 slice.274
  8.5 1.2 slice.275
  10.0 0.1 slice.278
  11.5 0.2 copy-done.3
  11.6 5.1 %fusion.5 = bf16[16,2,16,512]{3,2,0,1:T(8,128)(2,1)S(1)} fusion(f32[16,2,16,497]{3,2,1,0:T(8,128)S(1)} %slice.288, f32[16,2,16,498]{3,2,1,0:T(8,128)S(1)} %slice.287, f32[16,2,16,499]{3,2,1,0:T(8,128)S(1)} %slice.286, f32[16,2,16,500]{3,2,1,0:T(8,128)S(1)} %slice.285, f32[16,2,16,501]{3,2,1,0:T(8,128)S(1)} %slice.284, f32[16,2,16,502]{3,2,1,0:T(8,128)S(1)} %slice.283, ...), kind=kOutput, calls=%fused_computation.14 | convolution fusion | flops 109316096 | bytes 16536576 | tf_op jit(solution)/shard_map/aqcf,qcpk->apkf/dot_general | solution.py:51
  16.8 0.3 copy.53
  17.1 20.6 %all_to_all.23 = bf16[16,2,16,512]{3,0,1,2:T(8,128)(2,1)S(1)} all-to-all(bf16[16,2,16,512]{3,0,1,2:T(8,128)(2,1)S(1)} %copy.53), channel_id=1, replica_groups=mesh['grp'=2,'row'=4,'col'=2,'sub'=2] {'row'}, dimensions={2} | all-to-all | bytes 1048576 | tf_op jit(solution)/shard_map/all_to_all | solution.py:54
  37.7 0.8 copy.55
  38.6 0.8 dynamic_slice.7
  39.5 1.9 %gather_fusion = s32[256]{0:T(256)S(1)} fusion(s32[256]{0:T(256)S(1)} %copy-done, s32[1024]{0:T(1024)S(1)} %pad_clamp_fusion), kind=kCustom, calls=%fused_computation | custom fusion | bytes 3072 | tf_op jit(solution)/shard_map/gather | solution.py:70
  41.5 18.9 %all-gather.2.cloned.1.call-done = bf16[256,2,4,512]{3,0,2,1:T(8,128)(2,1)} async-done(((bf16[64,2,4,512]{3,0,2,1:T(8,128)(2,1)}), bf16[256,2,4,512]{3,0,2,1:T(8,128)(2,1)}) %all-gather.2.cloned.1.call-update) | async-done | bytes 2097168 | tf_op jit(solution)/shard_map/all_gather | solution.py:62
  60.4 2.8 %copy.56 = bf16[256,2,4,512]{0,3,2,1:T(8,128)(2,1)S(1)} copy(bf16[256,2,4,512]{3,0,2,1:T(8,128)(2,1)} %all-gather.2.cloned.1.call-done) | data formatting | bytes 4194304 | tf_op jit(solution)/shard_map/all_gather | solution.py:62
  63.2 0.7 fusion
  63.9 0.2 reshape.295
  64.2 0.5 fusion.74
  64.7 0.5 fusion.77
  65.1 0.5 subtract_bitcast_fusion
  65.6 0.5 add_bitcast_fusion
  66.1 0.7 fusion.1
  66.8 0.2 slice_bitcast_fusion.3
  67.1 1.6 %pad_maximum_fusion = bf16[4,64,2,4,512]{4,1,3,2,0:T(8,128)(2,1)} fusion(bf16[1,64,2,4,512]{4,1,3,2,0:T(8,128)(2,1)S(1)} %get-tuple-element.13, bf16[1,64,2,4,512]{4,1,3,2,0:T(8,128)(2,1)S(1)} %get-tuple-element.14, bf16[1,64,2,4,512]{4,1,3,2,0:T(8,128)(2,1)S(1)} %get-tuple-element.15, bf16[1,64,2,4,512]{4,1,3,2,0:T(8,128)(2,1)S(1)} %get-tuple-element.12), kind=kLoop, calls=%fused_computation.7 | loop fusion | flops 3145728 | bytes 4194304 | tf_op jit(solution)/shard_map/stack | solution.py:13
  68.6 4.6 %all-to-all-start.1 = ((bf16[4,64,2,4,512]{4,1,3,2,0:T(8,128)(2,1)}), bf16[4,64,2,4,512]{4,1,3,2,0:T(8,128)(2,1)S(1)}, u32[]{:S(2)}, u32[]{:S(2)}) async-start(bf16[4,64,2,4,512]{4,1,3,2,0:T(8,128)(2,1)} %pad_maximum_fusion), calls=%async_computation.1 | async-start | bytes 4194304 | tf_op jit(solution)/shard_map/all_to_all | solution.py:13
  73.3 0.1 fusion.76
  73.4 0.2 fusion.9
  73.6 0.1 fusion.75
  73.7 0.2 fusion.7
  73.9 0.6 copy.64
  74.5 47.3 %all-to-all-done.1 = bf16[4,64,2,4,512]{4,1,3,2,0:T(8,128)(2,1)S(1)} async-done(((bf16[4,64,2,4,512]{4,1,3,2,0:T(8,128)(2,1)}), bf16[4,64,2,4,512]{4,1,3,2,0:T(8,128)(2,1)S(1)}, u32[]{:S(2)}, u32[]{:S(2)}) %all-to-all-start.1) | async-done | bytes 2097184 | tf_op jit(solution)/shard_map/all_to_all | solution.py:13
  121.8 0.1 copy.62
  122.0 2.7 %convolution_bitcast_fusion = f32[64,2,16,512]{3,2,0,1:T(8,128)S(1)} fusion(bf16[64,2,16,512]{3,0,2,1:T(8,128)(2,1)S(1)} %bitcast.196, f32[1,2,16,16]{2,3,0,1:T(8,128)S(1)} %get-tuple-element.41, f32[1,2,16,16]{2,3,0,1:T(8,128)S(1)} %get-tuple-element.20), kind=kOutput, calls=%fused_computation.6 | convolution fusion | flops 402655232 | bytes 6295552 | tf_op jit(solution)/shard_map/bqkf,qkpc->bpcf/dot_general | solution.py:109
  124.7 17.3 %multiply_add_fusion = f32[64,2,16,512]{3,2,0,1:T(8,128)S(1)} fusion(f32[64,2,16,497]{3,2,0,1:T(8,128)S(1)} %bitcast.181, f32[64,2,16,498]{3,2,0,1:T(8,128)S(1)} %bitcast.182, f32[64,2,16,499]{3,2,0,1:T(8,128)S(1)} %bitcast.183, f32[64,2,16,500]{3,2,0,1:T(8,128)S(1)} %bitcast.184, f32[64,2,16,501]{3,2,0,1:T(8,128)S(1)} %bitcast.185, ...), kind=kLoop, calls=%fused_computation.5 | loop fusion | flops 32505856 | bytes 70321152 | tf_op jit(solution)/shard_map/add | solution.py:24
  142.0 2.6 %copy.65 = f32[64,2,16,512]{3,2,1,0:T(8,128)} copy(f32[64,2,16,512]{3,2,0,1:T(8,128)S(1)} %multiply_add_fusion) | data formatting | bytes 8388608
  (39 shorter events, 2.1 us)
Async XLA Ops:
  7.2 32.3 %copy-start = (s32[256]{0:T(256)S(1)}, s32[256]{0:T(256)}, u32[]{:S(2)}) copy-start(s32[256]{0:T(256)} %param.10) | copy-start | bytes 3076
  7.2 2.5 %copy-start.1 = (bf16[16,2,16,512]{3,2,1,0:T(8,128)(2,1)S(1)}, bf16[16,2,16,512]{3,2,1,0:T(8,128)(2,1)}, u32[]{:S(2)}) copy-start(bf16[16,2,16,512]{3,2,1,0:T(8,128)(2,1)} %param.7) | copy-start | bytes 1572868
  7.2 53.2 %all-gather.2.cloned.1.call-start = ((), (), s32[]{:S(2)}) async-start(), calls=%async_computation.2 | async-start | bytes 2621440 | tf_op jit(solution)/shard_map/all_gather | solution.py:62
  10.9 0.7 copy-start.3
  11.6 27.7 %copy-start.5 = (s32[32,1]{0,1:T(1,128)S(1)}, s32[32,1]{0,1:T(1,128)}, u32[]{:S(2)}) copy-start(s32[32,1]{0,1:T(1,128)} %param.11) | copy-start | bytes 388
  16.8 24.7 %copy-start.2 = (bf16[4,2,256,32]{2,3,1,0:T(8,128)(2,1)S(1)}, bf16[4,2,256,32]{2,3,1,0:T(8,128)(2,1)}, u32[]{:S(2)}) copy-start(bf16[4,2,256,32]{2,3,1,0:T(8,128)(2,1)} %param.13) | copy-start | bytes 393220
  67.1 6.2 %copy-start.4 = (f32[16,16]{1,0:T(8,128)S(1)}, f32[16,16]{1,0:T(8,128)}, u32[]{:S(2)}) copy-start(f32[16,16]{1,0:T(8,128)} %param.9) | copy-start | bytes 3076
  68.6 53.2 %all-to-all-start.1 = ((bf16[4,64,2,4,512]{4,1,3,2,0:T(8,128)(2,1)}), bf16[4,64,2,4,512]{4,1,3,2,0:T(8,128)(2,1)S(1)}, u32[]{:S(2)}, u32[]{:S(2)}) async-start(bf16[4,64,2,4,512]{4,1,3,2,0:T(8,128)(2,1)} %pad_maximum_fusion), calls=%async_computation.1 | async-start | bytes 4194304 | tf_op jit(solution)/shard_map/all_to_all | solution.py:13
Sparse Core Ops, SparseCore 0:
  38.7 21.6 all-gather.1
